TPU v7x, 32 devices: a whole 2x2x4 slice. The times are simulated.
32 devices in a mesh: groups: 2 (over y), wid: 8 (over z, x), hgt: 1, tp: 2 (over core).
Axes of the slice: x: 2, y: 2, z: 4, core: 2. Of those that a mesh axis runs over, the one named last changes fastest.
Arguments:
- self_query: bfloat16 [4, 8, 64, 2560], P('groups', 'hgt', 'wid', 'tp'), parts along dimension 0, may hold values from -250 to 250
- self_key: bfloat16 [4, 8, 64, 2560], P('groups', 'hgt', 'wid', 'tp'), parts along dimension 0, may hold values from -250 to 250
- self_value: bfloat16 [4, 8, 64, 2560], P('groups', 'hgt', 'wid', 'tp'), parts along dimension 0, may hold values from -6 to 6
- cross_query: bfloat16 [4, 8, 64, 2560], P('groups', 'hgt', 'wid', 'tp'), parts along dimension 0, may hold values from -250 to 250
- text_key: bfloat16 [1024, 2560], P(('groups', 'wid'), 'tp'), parts along dimension 0, may hold values from -25 to 25
- text_value: bfloat16 [1024, 2560], P(('groups', 'wid'), 'tp'), parts along dimension 0, may hold values from -6 to 6
- image_key: bfloat16 [514, 2560], P('groups', 'tp'), parts along dimension 0, may hold values from -25 to 25
- image_value: bfloat16 [514, 2560], P('groups', 'tp'), parts along dimension 0, may hold values from -6 to 6
- query_gain: float32 [2560], P('tp'), may hold values from 0.1 to 1.9
- key_gain: float32 [2560], P('tp'), may hold values from 0.1 to 1.9
- cross_gain: float32 [2560], P('tp'), may hold values from 0.1 to 1.9
- windows: int32 [20, 3], P('tp'), may hold values from 0 to 2, as said below
Outputs:
- self_out: bfloat16 [4, 8, 64, 2560], P('groups', 'hgt', 'wid', 'tp'), parts along dimension 0
- cross_out: bfloat16 [4, 8, 64, 2560], P('groups', 'hgt', 'wid', 'tp'), parts along dimension 0
There are 2 independent parts, one for each index of `groups`. A program takes and returns all parts, laid end to end along the dimension named above; an argument that names none is the same for every part. Nothing has to cross between parts.
Inputs may be any that keep to these rules, and one draw needn't show every extreme that they name: windows[n] holds head n's reach in frames, in height tiles and in width tiles; the last two are 0 or 1; some head has the reach (2, 1, 1).
All inputs are finite; a program needn't handle non-finite values.
Results may differ from a plain program's by a relative error of at most 0.0081.
Values may be sent and summed in bfloat16 or wider, within the bound.
A program may use at most 64 MiB of HBM per device.

v0:
```python
import math

import jax
import jax.numpy as jnp
from jax import lax
from jax.sharding import PartitionSpec as P

TILE = 4


epsilon = 1e-06
masked = -1e30


def padded(value, sides, width):
    for axis, dim in sides:
        count, length = (lax.axis_size(axis), value.shape[dim])
        up = [(i, (i + 1) % count) for i in range(count - 1)]
        down = [(j, i) for i, j in up]
        last = lax.slice_in_dim(value, length - width, length, axis=dim)
        first = lax.slice_in_dim(value, 0, width, axis=dim)
        before = lax.ppermute(last, axis, up)
        after = lax.ppermute(first, axis, down)
        value = jnp.concatenate([before, value, after], axis=dim)
    return value


def grid_positions(frame_count, row_count, col_count, row_start, col_start):
    full_shape = (frame_count, row_count, col_count)
    frame_ids = jnp.arange(frame_count, dtype=jnp.int32)[:, None, None]
    row_ids = jnp.arange(row_count, dtype=jnp.int32)[None, :, None] + row_start
    col_ids = jnp.arange(col_count, dtype=jnp.int32)[None, None, :] + col_start
    return (
        jnp.broadcast_to(frame_ids, full_shape).reshape(-1),
        jnp.broadcast_to(row_ids, full_shape).reshape(-1),
        jnp.broadcast_to(col_ids, full_shape).reshape(-1),
    )


def window_mask(windows, query_pos, key_pos, height_all, width_all):
    inside = (
        (key_pos[1] >= 0) & (key_pos[1] < height_all) & (key_pos[2] >= 0) & (key_pos[2] < width_all)
    )
    frame_gap = jnp.abs(query_pos[0][:, None] - key_pos[0][None, :])
    row_gap = jnp.abs(query_pos[1][:, None] // TILE - key_pos[1][None, :] // TILE)
    col_gap = jnp.abs(query_pos[2][:, None] // TILE - key_pos[2][None, :] // TILE)
    return (
        (frame_gap[None] <= windows[:, 0, None, None])
        & (row_gap[None] <= windows[:, 1, None, None])
        & (col_gap[None] <= windows[:, 2, None, None])
        & inside[None, None, :]
    )


def attend_part(queries, key_rows, value_rows, allowed):
    factor = 1.0 / math.sqrt(queries.shape[-1])
    scores = (
        jnp.einsum("qhd,khd->hqk", queries, key_rows, preferred_element_type=jnp.float32) * factor
    )
    if allowed is not None:
        scores = jnp.where(allowed, scores, masked)
    row_top = jnp.max(scores, axis=-1)
    powers = jnp.exp(scores - row_top[..., None])
    if allowed is not None:
        powers = jnp.where(allowed, powers, 0.0)
    weights = powers.astype(jnp.bfloat16)
    numerator = jnp.einsum("hqk,khd->hqd", weights, value_rows, preferred_element_type=jnp.float32)
    return (row_top, jnp.sum(powers, axis=-1), numerator)


def merge_parts(first, second):
    row_top = jnp.maximum(first[0], second[0])
    upper = jnp.exp(second[0] - row_top)
    return (row_top, second[1] * upper, second[2] * upper[..., None])


def finish_part(part, frame_count, row_count, col_count):
    heads_out = part[2] / part[1][..., None]
    return jnp.transpose(heads_out, (1, 0, 2)).reshape(frame_count, row_count, col_count, -1)


def sum_squares(field):
    wide = field.astype(jnp.float32)
    return jnp.sum(wide * wide, axis=-1)


def apply_norm(field, squares_all, channel_total, gain):
    inverse = lax.rsqrt(squares_all / channel_total + epsilon)
    return (field.astype(jnp.float32) * inverse[..., None] * gain).astype(jnp.bfloat16)


def flat_heads(field, head_count):
    return field.reshape(-1, head_count, field.shape[-1] // head_count)


def body(
    self_query,
    self_key,
    self_value,
    cross_query,
    text_key,
    text_value,
    image_key,
    image_value,
    query_gain,
    key_gain,
    cross_gain,
    windows,
):
    frame_count, row_count, col_count, channels = self_query.shape
    head_count = windows.shape[0]
    channel_total = channels * lax.axis_size("tp")
    height_all = row_count * lax.axis_size("hgt")
    width_all = col_count * lax.axis_size("wid")
    row_start = lax.axis_index("hgt") * row_count
    col_start = lax.axis_index("wid") * col_count
    squares_all = lax.psum(
        (sum_squares(self_query), sum_squares(self_key), sum_squares(cross_query)), "tp"
    )
    q_normed = apply_norm(self_query, squares_all[0], channel_total, query_gain)
    k_normed = apply_norm(self_key, squares_all[1], channel_total, key_gain)
    x_normed = apply_norm(cross_query, squares_all[2], channel_total, cross_gain)
    queries = flat_heads(q_normed, head_count)
    query_pos = grid_positions(frame_count, row_count, col_count, row_start, col_start)
    stacked = jnp.stack((k_normed, self_value))
    extended = padded(stacked, (("wid", 3), ("hgt", 2)), TILE)
    key_pos = grid_positions(
        frame_count, row_count + 2 * TILE, col_count + 2 * TILE, row_start - TILE, col_start - TILE
    )
    allowed = window_mask(windows, query_pos, key_pos, height_all, width_all)
    self_part = attend_part(
        queries, flat_heads(extended[0], head_count), flat_heads(extended[1], head_count), allowed
    )
    self_out = finish_part(self_part, frame_count, row_count, col_count).astype(jnp.bfloat16)
    crosses = flat_heads(x_normed, head_count)
    query_total = crosses.shape[0]
    start_part = (
        jnp.full((head_count, query_total), masked, jnp.float32),
        jnp.zeros((head_count, query_total), jnp.float32),
        jnp.zeros((head_count, query_total, crosses.shape[-1]), jnp.float32),
    )
    fresh = attend_part(
        crosses,
        flat_heads(lax.all_gather(text_key, "wid", axis=0, tiled=True), head_count),
        flat_heads(lax.all_gather(text_value, "wid", axis=0, tiled=True), head_count),
        None,
    )
    text_part = merge_parts(start_part, fresh)
    image_part = attend_part(
        crosses, flat_heads(image_key, head_count), flat_heads(image_value, head_count), None
    )
    cross_out = (
        finish_part(text_part, frame_count, row_count, col_count)
        + finish_part(image_part, frame_count, row_count, col_count)
    ).astype(jnp.bfloat16)
    return (self_out, cross_out)


def solution(mesh):
    in_specs = (
        P("groups", "hgt", "wid", "tp"),
        P("groups", "hgt", "wid", "tp"),
        P("groups", "hgt", "wid", "tp"),
        P("groups", "hgt", "wid", "tp"),
        P(("groups", "wid"), "tp"),
        P(("groups", "wid"), "tp"),
        P("groups", "tp"),
        P("groups", "tp"),
        P("tp"),
        P("tp"),
        P("tp"),
        P("tp", None),
    )
    out_specs = (P("groups", "hgt", "wid", "tp"), P("groups", "hgt", "wid", "tp"))
    return jax.shard_map(body, mesh=mesh, in_specs=in_specs, out_specs=out_specs, check_vma=False)
```

profile of v0, /device:TPU:0, one launch (start us, length us, event | category | flops | bytes accessed | tf_op | source)
XLA Modules:
  0.0 113.1 jit_solution(17763563721599846357)
XLA Ops:
  8.0 1.1 fusion.48
  9.1 1.2 %fusion.51 = f32[2,8,8]{2,1,0:T(8,128)S(1)} fusion(bf16[2,8,8,1280]{3,2,1,0:T(8,128)(2,1)} %param.13), kind=kLoop, calls=%fused_computation.47 | loop fusion | flops 491392 | bytes 328192 | tf_op jit(solution)/shard_map/reduce_sum | solution.py:84
  10.3 1.1 fusion.54
  11.4 3.7 %all-reduce = (f32[2,8,8]{2,1,0:T(8,128)S(1)}, f32[2,8,8]{2,1,0:T(8,128)S(1)}, f32[2,8,8]{2,1,0:T(8,128)S(1)}) all-reduce(f32[2,8,8]{2,1,0:T(8,128)S(1)} %fusion.51, f32[2,8,8]{2,1,0:T(8,128)S(1)} %fusion.48, f32[2,8,8]{2,1,0:T(8,128)S(1)} %fusion.54), channel_id=1, replica_groups=mesh['groups'=2,'wid'=8,'hgt'=1,'tp'=2] {'tp'}, use_global_device_ids=true, to_apply=%region_3.0 | all-reduce | flops 384 | bytes 3072 | tf_op jit(solution)/shard_map/psum | solution.py:117
  15.1 1.1 fusion.58
  16.3 2.2 %fusion.57 = (bf16[2,2,8,4,1280]{4,3,2,1,0:T(4,128)(2,1)}, bf16[2,2,8,4,1280]{4,3,2,1,0:T(4,128)(2,1)}) fusion(bf16[1,2,8,8,1280]{4,3,2,1,0:T(8,128)(2,1)S(1)} %fusion.58, bf16[1,2,8,8,1280]{4,3,2,1,0:T(8,128)(2,1)} %bitcast.51), kind=kLoop, calls=%fused_computation.55 | loop fusion | flops 1310720 | bytes 1310720 | tf_op jit(solution)/shard_map/stack | solution.py:125
  18.4 4.6 %collective-permute-start = (bf16[2,2,8,4,1280]{4,3,2,1,0:T(4,128)(2,1)}, bf16[2,2,8,4,1280]{4,3,2,1,0:T(4,128)(2,1)S(1)}, u32[]{:S(2)}, u32[]{:S(2)}) collective-permute-start(bf16[2,2,8,4,1280]{4,3,2,1,0:T(4,128)(2,1)} %get-tuple-element.9), channel_id=1, source_target_pairs={{0,2},{2,4},{4,6},{6,8},{8,10},{10,12},{12,14},{1,3},{3,5},{5,7},{... | collective-permute-start | bytes 983048 | tf_op jit(solution)/shard_map/ppermute | solution.py:22
  23.0 1.3 %collective-permute-start.1 = (bf16[2,2,8,4,1280]{4,3,2,1,0:T(4,128)(2,1)}, bf16[2,2,8,4,1280]{4,3,2,1,0:T(4,128)(2,1)}, u32[]{:S(2)}, u32[]{:S(2)}) collective-permute-start(bf16[2,2,8,4,1280]{4,3,2,1,0:T(4,128)(2,1)} %get-tuple-element.10), channel_id=1, source_target_pairs={{2,0},{4,2},{6,4},{8,6},{10,8},{12,10},{14,12},{3,1},{5,3},{7,5},{... | collective-permute-start | bytes 983048 | tf_op jit(solution)/shard_map/ppermute | solution.py:23
  24.8 0.9 fusion.50
  26.0 1.0 reshape.419
  27.4 1.6 %fusion.90 = (f32[10,128]{1,0:T(8,128)S(1)}, f32[10,128,257]{1,2,0:T(8,128)S(1)}) fusion(bf16[257,10,128]{2,1,0:T(8,128)(2,1)S(1)} %reshape.422, bf16[128,10,128]{2,1,0:T(8,128)(2,1)} %reshape.419), kind=kOutput, calls=%fused_computation.106 | convolution fusion | flops 84870400 | bytes 2306560 | tf_op jit(solution)/shard_map/qhd,khd->hqk/dot_general | solution.py:58
  29.1 8.8 %collective-permute-done = bf16[2,2,8,4,1280]{4,3,2,1,0:T(4,128)(2,1)S(1)} collective-permute-done((bf16[2,2,8,4,1280]{4,3,2,1,0:T(4,128)(2,1)}, bf16[2,2,8,4,1280]{4,3,2,1,0:T(4,128)(2,1)S(1)}, u32[]{:S(2)}, u32[]{:S(2)}) %collective-permute-start) | collective-permute-done | bytes 327712 | tf_op jit(solution)/shard_map/ppermute | solution.py:22
  37.8 1.7 %pad_maximum_fusion.1 = bf16[2,2,8,16,1280]{4,3,2,1,0:T(8,128)(2,1)S(1)} fusion(bf16[2,2,8,4,1280]{4,3,2,1,0:T(4,128)(2,1)} %collective-permute-done.1, bf16[1,2,8,8,1280]{4,3,2,1,0:T(8,128)(2,1)S(1)} %bitcast.52, bf16[1,2,8,8,1280]{4,3,2,1,0:T(8,128)(2,1)S(1)} %fusion.58, bf16[2,2,8,4,1280]{4,3,2,1,0:T(4,128)(2,1)S(1)} %collective-permute-done), kind=kLoop, calls=%fused_computation.13 | loop fusion | flops 5242880 | bytes 2621440 | tf_op jit(solution)/shard_map/concatenate | solution.py:24
  39.5 1.2 %fusion.84 = (bf16[2,2,4,16,1280]{4,3,2,1,0:T(8,128)(2,1)}, bf16[2,2,4,16,1280]{4,3,2,1,0:T(8,128)(2,1)}) fusion(bf16[2,2,8,16,1280]{4,3,2,1,0:T(8,128)(2,1)S(1)} %pad_maximum_fusion.1), kind=kLoop, calls=%fused_computation.104 | loop fusion | bytes 2621440 | tf_op jit(solution)/shard_map/slice | solution.py:20
  40.6 1.5 %collective-permute-start.2 = (bf16[2,2,4,16,1280]{4,3,2,1,0:T(8,128)(2,1)}, bf16[2,2,4,16,1280]{4,3,2,1,0:T(8,128)(2,1)}, u32[]{:S(2)}, u32[]{:S(2)}) collective-permute-start(bf16[2,2,4,16,1280]{4,3,2,1,0:T(8,128)(2,1)} %get-tuple-element.7), channel_id=1, source_target_pairs={} | collective-permute-start | bytes 1966088 | tf_op jit(solution)/shard_map/ppermute | solution.py:22
  42.1 1.5 %collective-permute-start.3 = (bf16[2,2,4,16,1280]{4,3,2,1,0:T(8,128)(2,1)}, bf16[2,2,4,16,1280]{4,3,2,1,0:T(8,128)(2,1)}, u32[]{:S(2)}, u32[]{:S(2)}) collective-permute-start(bf16[2,2,4,16,1280]{4,3,2,1,0:T(8,128)(2,1)} %get-tuple-element.8), channel_id=1, source_target_pairs={} | collective-permute-start | bytes 1966088 | tf_op jit(solution)/shard_map/ppermute | solution.py:23
  43.6 1.0 reshape.418
  44.8 1.4 %reshape.423 = bf16[257,10,128]{2,1,0:T(8,128)(2,1)} reshape(bf16[257,1280]{1,0:T(8,128)(2,1)S(1)} %copy-done.10) | data formatting | bytes 1315840 | tf_op jit(solution)/shard_map/reshape | solution.py:93
  46.4 0.8 subtract_abs_fusion.2
  47.3 0.9 subtract_abs_fusion
  48.2 2.1 %pad_maximum_fusion = bf16[2,2,16,16,1280]{4,3,2,1,0:T(8,128)(2,1)S(1)} fusion(bf16[2,2,4,16,1280]{4,3,2,1,0:T(8,128)(2,1)} %collective-permute-done.3, bf16[2,2,8,4,1280]{4,3,2,1,0:T(4,128)(2,1)} %collective-permute-done.1, bf16[1,2,8,8,1280]{4,3,2,1,0:T(8,128)(2,1)S(1)} %bitcast.53, bf16[1,2,8,8,1280]{4,3,2,1,0:T(8,128)(2,1)S(1)} %fusion.58, ...), kind=kLoop, calls=%fused_computation.1 | loop fusion | flops 15728640 | bytes 5242880 | tf_op jit(solution)/shard_map/concatenate | solution.py:24
  50.4 1.8 %reshape_squeeze.6 = bf16[512,10,128]{2,1,0:T(8,128)(2,1)} reshape(bf16[1,2,16,16,1280]{4,3,2,1,0:T(8,128)(2,1)S(1)} %get-tuple-element.5) | data formatting | bytes 2621440 | tf_op jit(solution)/shard_map/reshape;squeeze | solution.py:93
  52.2 1.8 %reshape_squeeze.7 = bf16[512,10,128]{2,1,0:T(8,128)(2,1)} reshape(bf16[1,2,16,16,1280]{4,3,2,1,0:T(8,128)(2,1)S(1)} %get-tuple-element.6) | data formatting | bytes 2621440 | tf_op jit(solution)/shard_map/reshape;squeeze | solution.py:93
  54.4 5.3 %fusion.85 = (f32[10,128]{1,0:T(8,128)S(1)}, bf16[10,128,512]{2,1,0:T(8,128)(2,1)}) fusion(bf16[512,10,128]{2,1,0:T(8,128)(2,1)S(1)} %copy-done.4, bf16[128,10,128]{2,1,0:T(8,128)(2,1)} %reshape.418, pred[512]{0:T(512)(128)(4,1)S(1)} %compare_and_fusion, s32[10]{0:T(128)S(1)} %get-tuple-element.14, s32[128,512]{1,0:T(8,128)} %get-tuple-element.24, ...), kind=kOutput, calls=%fused_computation.105 | convolution fusion | flops 179569152 | bytes 3741304 | tf_op jit(solution)/shard_map/sub | solution.py:63
  59.6 2.8 %fusion.36 = bf16[128,10,128]{2,0,1:T(8,128)(2,1)S(1)} fusion(bf16[512,10,128]{2,1,0:T(8,128)(2,1)} %reshape_squeeze.7, bf16[10,128,512]{2,1,0:T(8,128)(2,1)} %get-tuple-element.17, f32[128,10]{0,1:T(8,128)S(1)} %bitcast.56), kind=kOutput, calls=%fused_computation.31 | convolution fusion | flops 168099840 | bytes 2954240 | tf_op jit(solution)/shard_map/hqk,khd->hqd/dot_general | solution.py:67
  62.7 0.9 convert_element_type.48
  63.6 2.4 %copy.36 = bf16[512,1280]{0,1:T(8,128)(2,1)} copy(bf16[512,1280]{1,0:T(8,128)(2,1)} %all-gather.3.cloned.1.call-done) | data formatting | bytes 2621440 | tf_op jit(solution)/shard_map/all_gather | solution.py:144
  66.0 1.9 %multiply_reduce_fusion = (f32[10,128]{1,0:T(8,128)S(1)}, f32[10,128,512]{2,1,0:T(8,128)S(1)}) fusion(bf16[512,10,128]{0,2,1:T(8,128)(2,1)} %bitcast.50, bf16[128,10,128]{2,1,0:T(8,128)(2,1)S(1)} %copy-done.3), kind=kOutput, calls=%fused_computation.6 | convolution fusion | flops 169081600 | bytes 4264960 | tf_op jit(solution)/shard_map/qhd,khd->hqk/dot_general | solution.py:58
  68.7 31.0 %all-gather.5.cloned.1.call-done = bf16[512,1280]{1,0:T(8,128)(2,1)} async-done(((bf16[64,1280]{1,0:T(8,128)(2,1)}), bf16[512,1280]{1,0:T(8,128)(2,1)}) %all-gather.5.cloned.1.call-update) | async-done | bytes 1310736 | tf_op jit(solution)/shard_map/all_gather | solution.py:145
  99.7 2.4 %copy.39 = bf16[512,1280]{0,1:T(8,128)(2,1)} copy(bf16[512,1280]{1,0:T(8,128)(2,1)} %all-gather.5.cloned.1.call-done) | data formatting | bytes 2621440 | tf_op jit(solution)/shard_map/all_gather | solution.py:145
  102.1 2.2 %fusion.33 = f32[128,10,128]{2,0,1:T(8,128)S(1)} fusion(bf16[512,10,128]{0,2,1:T(8,128)(2,1)} %bitcast.54, f32[10,128,512]{2,1,0:T(8,128)S(1)} %get-tuple-element.19, f32[10,128]{1,0:T(8,128)S(1)} %get-tuple-element.18, f32[128,10]{0,1:T(8,128)S(1)} %get-tuple-element.12, f32[128,10]{0,1:T(8,128)S(1)} %get-tuple-element.11), kind=kOutput, calls=%fused_computation.30 | convolution fusion | flops 170065920 | bytes 4602880 | tf_op jit(solution)/shard_map/hqk,khd->hqd/dot_general | solution.py:67
  105.3 0.9 convert_element_type.54
  (68 shorter events, 4.7 us)
Async XLA Ops:
  7.2 17.6 %copy-start.5 = (bf16[2,8,8,1280]{3,2,1,0:T(8,128)(2,1)S(1)}, bf16[2,8,8,1280]{3,2,1,0:T(8,128)(2,1)}, u32[]{:S(2)}) copy-start(bf16[2,8,8,1280]{3,2,1,0:T(8,128)(2,1)} %param.12) | copy-start | bytes 983044
  7.2 18.6 %copy-start.6 = (bf16[2,8,8,1280]{3,2,1,0:T(8,128)(2,1)S(1)}, bf16[2,8,8,1280]{3,2,1,0:T(8,128)(2,1)}, u32[]{:S(2)}) copy-start(bf16[2,8,8,1280]{3,2,1,0:T(8,128)(2,1)} %param.15) | copy-start | bytes 983044
  7.2 17.6 %copy-start.13 = (s32[10,3]{0,1:T(4,128)S(1)}, s32[10,3]{0,1:T(4,128)}, u32[]{:S(2)}) copy-start(s32[10,3]{0,1:T(4,128)} %param.23) | copy-start | bytes 364
  7.2 17.6 %copy-start.11 = (f32[1280]{0:T(1024)S(1)}, f32[1280]{0:T(1024)}, u32[]{:S(2)}) copy-start(f32[1280]{0:T(1024)} %param.20) | copy-start | bytes 15364
  7.2 18.5 %copy-start.12 = (f32[1280]{0:T(1024)S(1)}, f32[1280]{0:T(1024)}, u32[]{:S(2)}) copy-start(f32[1280]{0:T(1024)} %param.22) | copy-start | bytes 15364
  7.2 56.4 %all-gather.3.cloned.1.call-start = ((), (), s32[]{:S(2)}) async-start(), calls=%async_computation | async-start | bytes 1474560 | tf_op jit(solution)/shard_map/all_gather | solution.py:144
  8.0 91.7 %all-gather.5.cloned.1.call-start = ((), (), s32[]{:S(2)}) async-start(), calls=%async_computation.1 | async-start | bytes 1474560 | tf_op jit(solution)/shard_map/all_gather | solution.py:145
  9.1 17.9 %copy-start.9 = (bf16[257,1280]{1,0:T(8,128)(2,1)S(1)}, bf16[257,1280]{1,0:T(8,128)(2,1)}, u32[]{:S(2)}) copy-start(bf16[257,1280]{1,0:T(8,128)(2,1)} %param.18) | copy-start | bytes 1973764
  18.4 19.4 %collective-permute-start = (bf16[2,2,8,4,1280]{4,3,2,1,0:T(4,128)(2,1)}, bf16[2,2,8,4,1280]{4,3,2,1,0:T(4,128)(2,1)S(1)}, u32[]{:S(2)}, u32[]{:S(2)}) collective-permute-start(bf16[2,2,8,4,1280]{4,3,2,1,0:T(4,128)(2,1)} %get-tuple-element.9), channel_id=1, source_target_pairs={{0,2},{2,4},{4,6},{6,8},{8,10},{10,12},{12,14},{1,3},{3,5},{5,7},{... | collective-permute-start | bytes 983048 | tf_op jit(solution)/shard_map/ppermute | solution.py:22
  23.0 14.8 %collective-permute-start.1 = (bf16[2,2,8,4,1280]{4,3,2,1,0:T(4,128)(2,1)}, bf16[2,2,8,4,1280]{4,3,2,1,0:T(4,128)(2,1)}, u32[]{:S(2)}, u32[]{:S(2)}) collective-permute-start(bf16[2,2,8,4,1280]{4,3,2,1,0:T(4,128)(2,1)} %get-tuple-element.10), channel_id=1, source_target_pairs={{2,0},{4,2},{6,4},{8,6},{10,8},{12,10},{14,12},{3,1},{5,3},{7,5},{... | collective-permute-start | bytes 983048 | tf_op jit(solution)/shard_map/ppermute | solution.py:23
  25.9 11.9 %copy-start.2 = (bf16[2,8,8,1280]{3,2,1,0:T(8,128)(2,1)S(1)}, bf16[2,8,8,1280]{3,2,1,0:T(8,128)(2,1)}, u32[]{:S(2)}) copy-start(bf16[2,8,8,1280]{3,2,1,0:T(8,128)(2,1)} %param.14) | copy-start | bytes 983044
  29.0 17.2 %copy-start = (f32[10,128,257]{1,2,0:T(8,128)}, f32[10,128,257]{1,2,0:T(8,128)S(1)}, u32[]{:S(2)}) copy-start(f32[10,128,257]{1,2,0:T(8,128)S(1)} %get-tuple-element.21) | copy-start | bytes 3947524
  29.0 14.6 %copy-start.7 = (bf16[2,8,8,1280]{3,2,1,0:T(8,128)(2,1)S(1)}, bf16[2,8,8,1280]{3,2,1,0:T(8,128)(2,1)}, u32[]{:S(2)}) copy-start(bf16[2,8,8,1280]{3,2,1,0:T(8,128)(2,1)} %fusion.50) | copy-start | bytes 983044
  29.0 15.7 %copy-start.10 = (bf16[257,1280]{1,0:T(8,128)(2,1)S(1)}, bf16[257,1280]{1,0:T(8,128)(2,1)}, u32[]{:S(2)}) copy-start(bf16[257,1280]{1,0:T(8,128)(2,1)} %param.19) | copy-start | bytes 1973764
  40.6 7.6 %collective-permute-start.2 = (bf16[2,2,4,16,1280]{4,3,2,1,0:T(8,128)(2,1)}, bf16[2,2,4,16,1280]{4,3,2,1,0:T(8,128)(2,1)}, u32[]{:S(2)}, u32[]{:S(2)}) collective-permute-start(bf16[2,2,4,16,1280]{4,3,2,1,0:T(8,128)(2,1)} %get-tuple-element.7), channel_id=1, source_target_pairs={} | collective-permute-start | bytes 1966088 | tf_op jit(solution)/shard_map/ppermute | solution.py:22
  42.1 6.1 %collective-permute-start.3 = (bf16[2,2,4,16,1280]{4,3,2,1,0:T(8,128)(2,1)}, bf16[2,2,4,16,1280]{4,3,2,1,0:T(8,128)(2,1)}, u32[]{:S(2)}, u32[]{:S(2)}) collective-permute-start(bf16[2,2,4,16,1280]{4,3,2,1,0:T(8,128)(2,1)} %get-tuple-element.8), channel_id=1, source_target_pairs={} | collective-permute-start | bytes 1966088 | tf_op jit(solution)/shard_map/ppermute | solution.py:23
  52.2 2.1 %copy-start.4 = (bf16[512,10,128]{2,1,0:T(8,128)(2,1)S(1)}, bf16[512,10,128]{2,1,0:T(8,128)(2,1)}, u32[]{:S(2)}) copy-start(bf16[512,10,128]{2,1,0:T(8,128)(2,1)} %reshape_squeeze.6) | copy-start | bytes 3932164
  62.4 3.6 %copy-start.3 = (bf16[128,10,128]{2,1,0:T(8,128)(2,1)S(1)}, bf16[128,10,128]{2,1,0:T(8,128)(2,1)}, u32[]{:S(2)}) copy-start(bf16[128,10,128]{2,1,0:T(8,128)(2,1)} %reshape.419) | copy-start | bytes 983044
  102.1 2.2 %copy-start.1 = (f32[10,128,257]{1,2,0:T(8,128)S(1)}, f32[10,128,257]{1,2,0:T(8,128)}, u32[]{:S(2)}) copy-start(f32[10,128,257]{1,2,0:T(8,128)} %copy-done) | copy-start | bytes 3947524
  102.1 2.2 %copy-start.8 = (bf16[257,10,128]{2,1,0:T(8,128)(2,1)S(1)}, bf16[257,10,128]{2,1,0:T(8,128)(2,1)}, u32[]{:S(2)}) copy-start(bf16[257,10,128]{2,1,0:T(8,128)(2,1)} %reshape.423) | copy-start | bytes 1973764
Sparse Core Ops, SparseCore 0:
  10.2 46.4 all-gather.2
  58.9 40.7 all-gather.4
where the time goes:
time: 114 us; the launch traced here: 113 us
  waiting for transfers between devices  40.4 us (35%)
  local copies, waits for them, and re-layouts  16.9 us (15%)
  matrix products  14.4 us (13%)
  between operations  14.4 us (13%)
  other arithmetic  14.3 us (13%)
  starting transfers between devices  8.92 us (8%)
  blocking collectives  3.69 us (3%)
    all_gather x1, waiting for transfers between devices, body(): lax.all_gather(text_value, 'wid', axis=0, tiled=True)  31 us
    ppermute x2, waiting for transfers between devices, padded(): before = lax.ppermute(last, axis, up)  8.76 us
    ppermute x2, starting transfers between devices, padded(): before = lax.ppermute(last, axis, up)  6.06 us
    dot_general x3, matrix products, attend_part(): jnp.einsum('hqk,khd->hqd', weights, value_rows, preferred_element_type=jn...  5.68 us
    sub x1, matrix products, attend_part(): powers = jnp.exp(scores - row_top[..., None])  5.26 us
    reshape x4, local copies, waits for them, and re-layouts, flat_heads(): return field.reshape(-1, head_count, field.shape[-1] // head_count)  3.85 us
    concatenate x2, other arithmetic, padded(): value = jnp.concatenate([before, value, after], axis=dim)  3.7 us
    psum x1, blocking collectives, body(): lax.psum((sum_squares(self_query), sum_squares(self_key), sum_squares(cro...  3.69 us
  transfers between devices with their start and end apart: 6, of which 2 were waited for; matrix products, arithmetic and copies ran while one was open for 34% of the time, Pallas kernels for 0%

commit v1 on v0

--- a/solution.py
+++ b/solution.py
@@ -1,8 +1,11 @@
+import functools
 import math
 
 import jax
 import jax.numpy as jnp
 from jax import lax
+from jax.experimental import pallas as pl
+from jax.experimental.pallas import tpu as pltpu
 from jax.sharding import PartitionSpec as P
 
 TILE = 4
@@ -156,6 +159,470 @@
     return (self_out, cross_out)
 
 
+MESH = pl.DeviceIdType.MESH
+
+
+def squares_of(ref, head_count, depth, tokens):
+    total = jnp.zeros((tokens, depth), jnp.float32)
+    for head in range(head_count):
+        wide = head_block(ref, head * depth, depth, tokens)
+        total = total + wide * wide
+    return jnp.sum(total, axis=-1, keepdims=True)
+
+
+def head_block(ref, start, depth, tokens):
+    block = ref[:, :, :, pl.ds(start, depth)]
+    return block.astype(jnp.float32).reshape(tokens, depth)
+
+
+def dot_nt(left, right):
+    return lax.dot_general(
+        left, right, (((1,), (1,)), ((), ())), preferred_element_type=jnp.float32
+    )
+
+
+def soft_mix(scores, value_rows, factor):
+    row_top = jnp.max(scores, axis=-1, keepdims=True)
+    powers = jnp.exp((scores - row_top) * factor)
+    total = jnp.sum(powers, axis=-1, keepdims=True)
+    mixed = jnp.dot(
+        powers.astype(jnp.bfloat16), value_rows, preferred_element_type=jnp.float32
+    )
+    return mixed * (1.0 / total)
+
+
+def fused(
+    wid_count,
+    head_count,
+    sq_ref,
+    sk_ref,
+    sv_ref,
+    xq_ref,
+    tk_ref,
+    tv_ref,
+    ik_ref,
+    iv_ref,
+    qg_ref,
+    kg_ref,
+    xg_ref,
+    win_ref,
+    so_ref,
+    co_ref,
+    text,
+    text_out,
+    keys,
+    values,
+    stat,
+    stat_in,
+    cross,
+    cross_send,
+    image_part,
+    back_send,
+    back_in,
+    gaps,
+    text_recv,
+    up_send,
+    down_send,
+    side_send,
+    halo_send,
+    halo_recv,
+    stat_send,
+    stat_recv,
+    cross_sem,
+    back_send_sem,
+    back_recv_sem,
+):
+    frames, rows, cols, channels = sq_ref.shape
+    tokens = frames * rows * cols
+    depth = channels // head_count
+    half_heads = head_count // 2
+    half = half_heads * depth
+    edge = frames * rows * TILE
+    col_tiles = cols // TILE
+    lines = wid_count // 2
+    factor = 1.0 / math.sqrt(depth)
+
+    w = lax.axis_index("wid")
+    core = lax.axis_index("tp")
+    line = w // 2
+    side = w % 2
+    mate = line * 2 + (1 - side)
+    not_first, not_last = w > 0, w < wid_count - 1
+    has_down, has_up = line > 0, line < lines - 1
+
+    def at_wid(target):
+        return {"wid": target}
+
+    barrier = pltpu.get_barrier_semaphore()
+    pl.semaphore_signal(barrier, inc=1, device_id={"tp": 1 - core}, device_id_type=MESH)
+    for cond, target in (
+        (not_first, w - 1),
+        (not_last, w + 1),
+        (has_down, w - 2),
+        (has_up, w + 2),
+    ):
+
+        @pl.when(cond)
+        def _():
+            pl.semaphore_signal(barrier, inc=1, device_id=at_wid(target), device_id_type=MESH)
+
+    mine = pl.multiple_of(side * half, depth)
+    other = pl.multiple_of((1 - side) * half, depth)
+    text[w, 0] = tk_ref[:, pl.ds(mine, half)]
+    text[w, 1] = tv_ref[:, pl.ds(mine, half)]
+    text_out[0] = tk_ref[:, pl.ds(other, half)]
+    text_out[1] = tv_ref[:, pl.ds(other, half)]
+    expected = 1
+    for cond in (not_first, not_last, has_down, has_up):
+        expected = expected + jnp.where(cond, 1, 0)
+    pl.semaphore_wait(barrier, expected)
+
+    def relay(slot, up):
+        return pltpu.make_async_remote_copy(
+            src_ref=text.at[slot],
+            dst_ref=text.at[slot],
+            send_sem=(up_send if up else down_send).at[slot],
+            recv_sem=text_recv.at[slot],
+            device_id=at_wid(w + 2 if up else w - 2),
+            device_id_type=MESH,
+        )
+
+    def forward(slot, up):
+        @pl.when(has_up if up else has_down)
+        def _():
+            relay(slot, up).start()
+
+    def take(slot):
+        pltpu.make_async_remote_copy(
+            src_ref=text.at[slot],
+            dst_ref=text.at[slot],
+            send_sem=side_send,
+            recv_sem=text_recv.at[slot],
+            device_id=at_wid(mate),
+            device_id_type=MESH,
+        ).wait_recv()
+
+    def relay_step(step, which):
+        below, above = (line - step) * 2 + which, (line + step) * 2 + which
+
+        @pl.when(line - step >= 0)
+        def _():
+            take(below)
+            forward(below, True)
+
+        @pl.when(line + step < lines)
+        def _():
+            take(above)
+            forward(above, False)
+
+    forward(w, True)
+    forward(w, False)
+    side_copy = pltpu.make_async_remote_copy(
+        src_ref=text_out,
+        dst_ref=text.at[w],
+        send_sem=side_send,
+        recv_sem=text_recv.at[w],
+        device_id=at_wid(mate),
+        device_id_type=MESH,
+    )
+    side_copy.start()
+
+    lane = lax.broadcasted_iota(jnp.int32, (tokens, depth), 1)
+    sums = [squares_of(ref, head_count, depth, tokens) for ref in (sq_ref, sk_ref, xq_ref)]
+    stat[...] = jnp.where(lane == 0, sums[0], jnp.where(lane == 1, sums[1], sums[2]))
+    stat_copy = pltpu.make_async_remote_copy(
+        src_ref=stat,
+        dst_ref=stat_in,
+        send_sem=stat_send,
+        recv_sem=stat_recv,
+        device_id={"tp": 1 - core},
+        device_id_type=MESH,
+    )
+    stat_copy.start()
+
+    place = lax.broadcasted_iota(jnp.int32, (tokens, tokens), 0)
+    source = lax.broadcasted_iota(jnp.int32, (tokens, tokens), 1)
+    inner = lax.rem(place, edge)
+    natural = (
+        lax.div(inner, rows * TILE) * (rows * cols)
+        + lax.rem(lax.div(inner, TILE), rows) * cols
+        + lax.div(place, edge) * TILE
+        + lax.rem(inner, TILE)
+    )
+    to_tiles = jnp.where(natural == source, 1.0, 0.0).astype(jnp.bfloat16)
+
+    def tile_order(block):
+        return jnp.dot(to_tiles, block, preferred_element_type=jnp.float32).astype(jnp.bfloat16)
+
+    def halo(ref, at, down):
+        return pltpu.make_async_remote_copy(
+            src_ref=ref.at[pl.ds(edge if down else tokens, edge)],
+            dst_ref=ref.at[pl.ds(edge + tokens if down else 0, edge)],
+            send_sem=halo_send.at[at],
+            recv_sem=halo_recv.at[at],
+            device_id=at_wid(w - 1 if down else w + 1),
+            device_id_type=MESH,
+        )
+
+    def start_halo(ref, at):
+        @pl.when(not_first)
+        def _():
+            halo(ref, at, True).start()
+
+        @pl.when(not_last)
+        def _():
+            halo(ref, at + 1, False).start()
+
+    @pl.when(w == 0)
+    def _():
+        for ref in (keys, values):
+            ref[0:edge] = jnp.zeros((edge, channels), jnp.bfloat16)
+
+    @pl.when(w == wid_count - 1)
+    def _():
+        for ref in (keys, values):
+            ref[edge + tokens :] = jnp.zeros((edge, channels), jnp.bfloat16)
+
+    for head in range(head_count):
+        block = head_block(sv_ref, head * depth, depth, tokens).astype(jnp.bfloat16)
+        values[edge : edge + tokens, head * depth : (head + 1) * depth] = tile_order(block)
+    start_halo(values, 2)
+
+    stat_copy.wait()
+    whole = stat[...] + stat_in[...]
+    inverse = lax.rsqrt(whole / (channels * 2) + epsilon)
+    inverse_q, inverse_k, inverse_x = inverse[:, 0:1], inverse[:, 1:2], inverse[:, 2:3]
+
+    def normed(ref, gain_ref, start, inverse_of):
+        wide = head_block(ref, start, depth, tokens)
+        return (wide * inverse_of * gain_ref[:, pl.ds(start, depth)]).astype(jnp.bfloat16)
+
+    for head in range(head_count):
+        block = normed(sk_ref, kg_ref, head * depth, inverse_k)
+        keys[edge : edge + tokens, head * depth : (head + 1) * depth] = tile_order(block)
+    start_halo(keys, 0)
+
+    for head in range(half_heads):
+        at = pl.multiple_of((1 - side) * half + head * depth, depth)
+        cross_send[:, head * depth : (head + 1) * depth] = normed(xq_ref, xg_ref, at, inverse_x)
+    cross_copy = pltpu.make_async_remote_copy(
+        src_ref=cross_send,
+        dst_ref=cross.at[pl.ds(tokens, tokens)],
+        send_sem=cross_sem.at[0],
+        recv_sem=cross_sem.at[1],
+        device_id=at_wid(mate),
+        device_id_type=MESH,
+    )
+    cross_copy.start()
+
+    take(mate)
+    forward(mate, True)
+    forward(mate, False)
+
+    for head in range(half_heads):
+        at = pl.multiple_of(side * half + head * depth, depth)
+        cross[0:tokens, head * depth : (head + 1) * depth] = normed(xq_ref, xg_ref, at, inverse_x)
+
+    spread = (tokens, tokens + 2 * edge)
+    query = lax.broadcasted_iota(jnp.int32, spread, 0)
+    key = lax.broadcasted_iota(jnp.int32, spread, 1)
+    key_tile = lax.div(key, edge) - 1
+    key_inner = lax.rem(key, edge)
+    key_col = key_tile + w * col_tiles
+    inside = (key_col >= 0) & (key_col < wid_count * col_tiles)
+    frame_gap = jnp.abs(lax.div(query, rows * cols) - lax.div(key_inner, rows * TILE))
+    row_gap = jnp.abs(
+        lax.div(lax.rem(lax.div(query, cols), rows), TILE)
+        - lax.div(lax.rem(lax.div(key_inner, TILE), rows), TILE)
+    )
+    col_gap = jnp.abs(lax.div(lax.rem(query, cols), TILE) - key_tile)
+    gaps[0] = jnp.where(inside, frame_gap, 1 << 30)
+    gaps[1] = row_gap
+    gaps[2] = col_gap
+
+    def self_head(head):
+        at = slice(head * depth, (head + 1) * depth)
+        queries = normed(sq_ref, qg_ref, head * depth, inverse_q)
+        scores = dot_nt(queries, keys[:, at])
+        allowed = (
+            (gaps[0] <= win_ref[head, 0])
+            & (gaps[1] <= win_ref[head, 1])
+            & (gaps[2] <= win_ref[head, 2])
+        )
+        mixed = soft_mix(jnp.where(allowed, scores, masked), values[:, at], factor)
+        so_ref[:, :, :, at] = mixed.reshape(frames, rows, cols, depth).astype(jnp.bfloat16)
+
+    def image_head(head):
+        at = slice(head * depth, (head + 1) * depth)
+        there = pl.ds(pl.multiple_of(side * half + head * depth, depth), depth)
+        scores = dot_nt(cross[:, at], ik_ref[:, there])
+        image_part[:, at] = soft_mix(scores, iv_ref[:, there], factor)
+
+    cross_copy.wait_recv()
+    steps = [(step, turn) for step in range(1, lines) for turn in range(2)]
+
+    def next_step():
+        if steps:
+            step, turn = steps.pop(0)
+            relay_step(step, side if turn == 0 else 1 - side)
+
+    next_step()
+    for head in range(half_heads):
+        image_head(head)
+        if head == half_heads // 2:
+            next_step()
+    next_step()
+
+    def wait_halo(ref, at):
+        @pl.when(not_last)
+        def _():
+            halo(ref, at, True).wait_recv()
+
+        @pl.when(not_first)
+        def _():
+            halo(ref, at + 1, False).wait_recv()
+
+    wait_halo(values, 2)
+    wait_halo(keys, 0)
+    for head in range(head_count):
+        self_head(head)
+        if head == head_count // 2 - 1:
+            next_step()
+    while steps:
+        next_step()
+
+    backs = []
+    for head in range(half_heads):
+        at = slice(head * depth, (head + 1) * depth)
+        rows_all = wid_count * tk_ref.shape[0]
+        scores = dot_nt(cross[:, at], text[:, 0, :, at].reshape(rows_all, depth))
+        mixed = soft_mix(scores, text[:, 1, :, at].reshape(rows_all, depth), factor)
+        mixed = mixed + image_part[:, at]
+        back_send[head] = mixed[tokens:].astype(jnp.bfloat16)
+        back = pltpu.make_async_remote_copy(
+            src_ref=back_send.at[head],
+            dst_ref=back_in.at[head],
+            send_sem=back_send_sem.at[head],
+            recv_sem=back_recv_sem.at[head],
+            device_id=at_wid(mate),
+            device_id_type=MESH,
+        )
+        back.start()
+        backs.append(back)
+        there = pl.ds(pl.multiple_of(side * half + head * depth, depth), depth)
+        own = mixed[:tokens].reshape(frames, rows, cols, depth)
+        co_ref[:, :, :, there] = own.astype(jnp.bfloat16)
+
+    side_copy.wait_send()
+    cross_copy.wait_send()
+    for at, ref in ((0, keys), (2, values)):
+
+        @pl.when(not_first)
+        def _():
+            halo(ref, at, True).wait_send()
+
+        @pl.when(not_last)
+        def _():
+            halo(ref, at + 1, False).wait_send()
+
+    for place_line in range(lines):
+        for place_side in range(2):
+            slot = place_line * 2 + place_side
+
+            @pl.when(has_up & (place_line <= line))
+            def _():
+                relay(slot, True).wait_send()
+
+            @pl.when(has_down & (place_line >= line))
+            def _():
+                relay(slot, False).wait_send()
+
+    for head in range(half_heads):
+        backs[head].wait()
+        there = pl.ds(pl.multiple_of((1 - side) * half + head * depth, depth), depth)
+        came = back_in[head].astype(jnp.float32).reshape(frames, rows, cols, depth)
+        co_ref[:, :, :, there] = came.astype(jnp.bfloat16)
+
+
+def fused_body(
+    wid_count,
+    self_query,
+    self_key,
+    self_value,
+    cross_query,
+    text_key,
+    text_value,
+    image_key,
+    image_value,
+    query_gain,
+    key_gain,
+    cross_gain,
+    windows,
+):
+    frames, rows, cols, channels = self_query.shape
+    tokens = frames * rows * cols
+    head_count = windows.shape[0]
+    depth = channels // head_count
+    half_heads = head_count // 2
+    half = half_heads * depth
+    edge = frames * rows * TILE
+    text_rows = text_key.shape[0]
+    bf16, f32 = jnp.bfloat16, jnp.float32
+    dma = pltpu.SemaphoreType.DMA
+    vmem = pl.BlockSpec(memory_space=pltpu.VMEM)
+    return pl.pallas_call(
+        functools.partial(fused, wid_count, head_count),
+        out_shape=(
+            jax.ShapeDtypeStruct(self_query.shape, bf16),
+            jax.ShapeDtypeStruct(self_query.shape, bf16),
+        ),
+        in_specs=[vmem] * 11 + [pl.BlockSpec(memory_space=pltpu.SMEM)],
+        out_specs=(vmem, vmem),
+        scratch_shapes=[
+            pltpu.VMEM((wid_count, 2, text_rows, half), bf16),
+            pltpu.VMEM((2, text_rows, half), bf16),
+            pltpu.VMEM((tokens + 2 * edge, channels), bf16),
+            pltpu.VMEM((tokens + 2 * edge, channels), bf16),
+            pltpu.VMEM((tokens, depth), f32),
+            pltpu.VMEM((tokens, depth), f32),
+            pltpu.VMEM((2 * tokens, half), bf16),
+            pltpu.VMEM((tokens, half), bf16),
+            pltpu.VMEM((2 * tokens, half), f32),
+            pltpu.VMEM((half_heads, tokens, depth), bf16),
+            pltpu.VMEM((half_heads, tokens, depth), bf16),
+            pltpu.VMEM((3, tokens, tokens + 2 * edge), jnp.int32),
+            dma((wid_count,)),
+            dma((wid_count,)),
+            dma((wid_count,)),
+            dma,
+            dma((4,)),
+            dma((4,)),
+            dma,
+            dma,
+            dma((2,)),
+            dma((half_heads,)),
+            dma((half_heads,)),
+        ],
+        compiler_params=pltpu.CompilerParams(
+            collective_id=0, has_side_effects=True, vmem_limit_bytes=40 * 1024 * 1024
+        ),
+        name="attention",
+    )(
+        self_query,
+        self_key,
+        self_value,
+        cross_query,
+        text_key,
+        text_value,
+        image_key,
+        image_value,
+        query_gain[None],
+        key_gain[None],
+        cross_gain[None],
+        windows,
+    )
+
+
 def solution(mesh):
     in_specs = (
         P("groups", "hgt", "wid", "tp"),
@@ -172,4 +639,13 @@
         P("tp", None),
     )
     out_specs = (P("groups", "hgt", "wid", "tp"), P("groups", "hgt", "wid", "tp"))
-    return jax.shard_map(body, mesh=mesh, in_specs=in_specs, out_specs=out_specs, check_vma=False)
+
+    def chosen(*args):
+        wid_count = mesh.shape["wid"]
+        one_row = mesh.shape["hgt"] == 1 and mesh.shape["tp"] == 2
+        even = wid_count % 2 == 0 and args[-1].shape[0] % 2 == 0
+        if one_row and even:
+            return fused_body(wid_count, *args)
+        return body(*args)
+
+    return jax.shard_map(chosen, mesh=mesh, in_specs=in_specs, out_specs=out_specs, check_vma=False)

time: 114 us -> 60 us (0.53)
  Pallas kernels: 0 us -> 47.3 us
  waiting for transfers between devices: 40.4 us -> 0 us
  matrix products: 14.4 us -> 0 us
  other arithmetic: 14.3 us -> 0 us
  between operations: 14.4 us -> 0.67 us
  starting transfers between devices: 8.92 us -> 0 us
  local copies, waits for them, and re-layouts: 16.9 us -> 11.5 us
  blocking collectives: 3.69 us -> 0 us
    pallas_call x0 -> x1, Pallas kernels: none -> 47.3 us  [fused_body(): pl.pallas_call(functools.partial(fused, wid_count, head_count), out_shape...]
    all_gather x2 -> x0, waiting for transfers between devices: 31 us -> none  [the longest x1 31 us: body(): lax.all_gather(text_value, 'wid', axis=0, tiled=True)]
    unnamed x28 -> x25, local copies, waits for them, and re-layouts: 0.38 us -> 10.8 us
    dot_general x5 -> x0, matrix products: 9.16 us -> none  [the longest x3 5.68 us: attend_part(): jnp.einsum('hqk,khd->hqd', weights, value_rows, preferred_element_type=jn...]
    ppermute x4 -> x0, starting transfers between devices: 8.84 us -> none  [the longest x2 6.06 us: padded(): before = lax.ppermute(last, axis, up)]
    ppermute x4 -> x0, waiting for transfers between devices: 8.76 us -> none  [the longest x2 8.76 us: padded(): before = lax.ppermute(last, axis, up)]
    sub x1 -> x0, matrix products: 5.26 us -> none  [attend_part(): powers = jnp.exp(scores - row_top[..., None])]
    all_gather x2 -> x0, local copies, waits for them, and re-layouts: 4.85 us -> none  [the longest x1 2.43 us: body(): lax.all_gather(text_key, 'wid', axis=0, tiled=True)]
  transfers between devices with their start and end apart: 6 -> 0, of which waited for: 2 -> 0; matrix products, arithmetic and copies ran while one was open for 34% -> 0% of each run, Pallas kernels for 0% -> 0%
where the time goes in v1:
time: 60 us; the launch traced here: 59.5 us
  Pallas kernels  47.3 us (79%)
  local copies, waits for them, and re-layouts  11.5 us (19%)
  between operations  0.67 us (1%)
    pallas_call x1, Pallas kernels, fused_body(): pl.pallas_call(functools.partial(fused, wid_count, head_count), out_shape...  47.3 us
    unnamed x25, local copies, waits for them, and re-layouts  10.8 us

profile of v1, /device:TPU:0, one launch (start us, length us, event | category | flops | bytes accessed | tf_op | source)
XLA Modules:
  0.0 59.5 jit_solution(17959329153223807873)
XLA Ops:
  0.6 0.0 copy-start.8
  0.6 0.7 %broadcast_in_dim.9.qg_ref = f32[1,1280]{1,0:T(1,128)S(1)} reshape(f32[1280]{0:T(1024)} %param.20) | data formatting | bytes 10240 | tf_op jit(solution)/shard_map/broadcast_in_dim | solution.py:619
  1.3 0.0 copy-done.8
  1.4 0.0 copy-start.9
  1.4 0.7 %copy-done.9 = f32[1280]{0:T(1024)S(1)} copy-done((f32[1280]{0:T(1024)S(1)}, f32[1280]{0:T(1024)}, u32[]{:S(2)}) %copy-start.9) | copy-done | bytes 5144
  2.0 0.0 copy-start.10
  2.1 0.7 %copy-done.10 = s32[10,3]{0,1:T(4,128)S(1)} copy-done((s32[10,3]{0,1:T(4,128)S(1)}, s32[10,3]{0,1:T(4,128)}, u32[]{:S(2)}) %copy-start.10) | copy-done | bytes 144
  2.7 0.1 copy.14.win_ref
  2.8 0.0 copy-start
  2.8 1.1 %copy-done = bf16[257,1280]{1,0:T(8,128)(2,1)S(1)} copy-done((bf16[257,1280]{1,0:T(8,128)(2,1)S(1)}, bf16[257,1280]{1,0:T(8,128)(2,1)}, u32[]{:S(2)}) %copy-start) | copy-done | bytes 657944
  3.9 0.0 copy-start.1
  3.9 1.1 %copy-done.1 = bf16[257,1280]{1,0:T(8,128)(2,1)S(1)} copy-done((bf16[257,1280]{1,0:T(8,128)(2,1)S(1)}, bf16[257,1280]{1,0:T(8,128)(2,1)}, u32[]{:S(2)}) %copy-start.1) | copy-done | bytes 657944
  5.0 0.0 copy-start.2
  5.0 1.0 %copy-done.2 = bf16[2,8,8,1280]{3,2,1,0:T(8,128)(2,1)S(1)} copy-done((bf16[2,8,8,1280]{3,2,1,0:T(8,128)(2,1)S(1)}, bf16[2,8,8,1280]{3,2,1,0:T(8,128)(2,1)}, u32[]{:S(2)}) %copy-start.2) | copy-done | bytes 327704
  6.0 0.0 copy-start.3
  6.0 1.0 %copy-done.3 = bf16[2,8,8,1280]{3,2,1,0:T(8,128)(2,1)S(1)} copy-done((bf16[2,8,8,1280]{3,2,1,0:T(8,128)(2,1)S(1)}, bf16[2,8,8,1280]{3,2,1,0:T(8,128)(2,1)}, u32[]{:S(2)}) %copy-start.3) | copy-done | bytes 327704
  7.0 0.0 copy-start.4
  7.0 1.0 %copy-done.4 = bf16[2,8,8,1280]{3,2,1,0:T(8,128)(2,1)S(1)} copy-done((bf16[2,8,8,1280]{3,2,1,0:T(8,128)(2,1)S(1)}, bf16[2,8,8,1280]{3,2,1,0:T(8,128)(2,1)}, u32[]{:S(2)}) %copy-start.4) | copy-done | bytes 327704
  7.9 0.0 copy-start.5
  7.9 1.0 %copy-done.5 = bf16[2,8,8,1280]{3,2,1,0:T(8,128)(2,1)S(1)} copy-done((bf16[2,8,8,1280]{3,2,1,0:T(8,128)(2,1)S(1)}, bf16[2,8,8,1280]{3,2,1,0:T(8,128)(2,1)}, u32[]{:S(2)}) %copy-start.5) | copy-done | bytes 327704
  8.9 0.0 copy-start.6
  8.9 0.9 %copy-done.6 = bf16[64,1280]{1,0:T(8,128)(2,1)S(1)} copy-done((bf16[64,1280]{1,0:T(8,128)(2,1)S(1)}, bf16[64,1280]{1,0:T(8,128)(2,1)}, u32[]{:S(2)}) %copy-start.6) | copy-done | bytes 163864
  9.8 0.0 copy-start.7
  9.8 0.9 %copy-done.7 = bf16[64,1280]{1,0:T(8,128)(2,1)S(1)} copy-done((bf16[64,1280]{1,0:T(8,128)(2,1)S(1)}, bf16[64,1280]{1,0:T(8,128)(2,1)}, u32[]{:S(2)}) %copy-start.7) | copy-done | bytes 163864
  10.7 47.3 %attention.1 = (bf16[2,8,8,1280]{3,2,1,0:T(8,128)(2,1)S(1)}, bf16[2,8,8,1280]{3,2,1,0:T(8,128)(2,1)S(1)}) custom-call(bf16[2,8,8,1280]{3,2,1,0:T(8,128)(2,1)S(1)} %copy-done.2, bf16[2,8,8,1280]{3,2,1,0:T(8,128)(2,1)S(1)} %copy-done.3, bf16[2,8,8,1280]{3,2,1,0:T(8,128)(2,1)S(1)} %copy-done.4, bf16[2,8,8,1280]{3,2,1,0:T(8,128)(2,1)S(1)} %copy-done.5, ...), custom_call_target="tpu_custom_call" | custom-call | tf_op jit(solution)/shard_map/attention/pallas_call | solution.py:573
  58.1 0.7 %copy.17 = bf16[2,8,8,1280]{3,2,1,0:T(8,128)(2,1)} copy(bf16[2,8,8,1280]{3,2,1,0:T(8,128)(2,1)S(1)} %get-tuple-element.4) | data formatting | bytes 655360
  58.8 0.7 %copy.18 = bf16[2,8,8,1280]{3,2,1,0:T(8,128)(2,1)} copy(bf16[2,8,8,1280]{3,2,1,0:T(8,128)(2,1)S(1)} %get-tuple-element.5) | data formatting | bytes 655360
  (2 shorter events, 0.0 us)
Async XLA Ops:
  0.6 0.7 %copy-start.8 = (f32[1280]{0:T(1024)S(1)}, f32[1280]{0:T(1024)}, u32[]{:S(2)}) copy-start(f32[1280]{0:T(1024)} %param.21) | copy-start | bytes 15364
  1.4 0.7 %copy-start.9 = (f32[1280]{0:T(1024)S(1)}, f32[1280]{0:T(1024)}, u32[]{:S(2)}) copy-start(f32[1280]{0:T(1024)} %param.22) | copy-start | bytes 15364
  2.0 0.7 %copy-start.10 = (s32[10,3]{0,1:T(4,128)S(1)}, s32[10,3]{0,1:T(4,128)}, u32[]{:S(2)}) copy-start(s32[10,3]{0,1:T(4,128)} %param.23) | copy-start | bytes 364
  2.8 1.1 %copy-start = (bf16[257,1280]{1,0:T(8,128)(2,1)S(1)}, bf16[257,1280]{1,0:T(8,128)(2,1)}, u32[]{:S(2)}) copy-start(bf16[257,1280]{1,0:T(8,128)(2,1)} %ik_ref.1) | copy-start | bytes 1973764
  3.9 1.1 %copy-start.1 = (bf16[257,1280]{1,0:T(8,128)(2,1)S(1)}, bf16[257,1280]{1,0:T(8,128)(2,1)}, u32[]{:S(2)}) copy-start(bf16[257,1280]{1,0:T(8,128)(2,1)} %iv_ref.1) | copy-start | bytes 1973764
  5.0 1.0 %copy-start.2 = (bf16[2,8,8,1280]{3,2,1,0:T(8,128)(2,1)S(1)}, bf16[2,8,8,1280]{3,2,1,0:T(8,128)(2,1)}, u32[]{:S(2)}) copy-start(bf16[2,8,8,1280]{3,2,1,0:T(8,128)(2,1)} %sq_ref.1) | copy-start | bytes 983044
  6.0 1.0 %copy-start.3 = (bf16[2,8,8,1280]{3,2,1,0:T(8,128)(2,1)S(1)}, bf16[2,8,8,1280]{3,2,1,0:T(8,128)(2,1)}, u32[]{:S(2)}) copy-start(bf16[2,8,8,1280]{3,2,1,0:T(8,128)(2,1)} %sk_ref.1) | copy-start | bytes 983044
  7.0 1.0 %copy-start.4 = (bf16[2,8,8,1280]{3,2,1,0:T(8,128)(2,1)S(1)}, bf16[2,8,8,1280]{3,2,1,0:T(8,128)(2,1)}, u32[]{:S(2)}) copy-start(bf16[2,8,8,1280]{3,2,1,0:T(8,128)(2,1)} %sv_ref.1) | copy-start | bytes 983044
  7.9 1.0 %copy-start.5 = (bf16[2,8,8,1280]{3,2,1,0:T(8,128)(2,1)S(1)}, bf16[2,8,8,1280]{3,2,1,0:T(8,128)(2,1)}, u32[]{:S(2)}) copy-start(bf16[2,8,8,1280]{3,2,1,0:T(8,128)(2,1)} %xq_ref.1) | copy-start | bytes 983044
  8.9 0.9 %copy-start.6 = (bf16[64,1280]{1,0:T(8,128)(2,1)S(1)}, bf16[64,1280]{1,0:T(8,128)(2,1)}, u32[]{:S(2)}) copy-start(bf16[64,1280]{1,0:T(8,128)(2,1)} %tk_ref.1) | copy-start | bytes 491524
  9.8 0.9 %copy-start.7 = (bf16[64,1280]{1,0:T(8,128)(2,1)S(1)}, bf16[64,1280]{1,0:T(8,128)(2,1)}, u32[]{:S(2)}) copy-start(bf16[64,1280]{1,0:T(8,128)(2,1)} %tv_ref.1) | copy-start | bytes 491524

commit v2 on v1

--- a/solution.py
+++ b/solution.py
@@ -194,20 +194,31 @@
 def fused(
     wid_count,
     head_count,
+    sq_hbm,
+    sk_hbm,
+    sv_hbm,
+    xq_hbm,
+    tk_hbm,
+    tv_hbm,
+    ik_hbm,
+    iv_hbm,
+    qg_hbm,
+    kg_hbm,
+    xg_hbm,
+    win_ref,
+    so_ref,
+    co_ref,
     sq_ref,
     sk_ref,
     sv_ref,
     xq_ref,
-    tk_ref,
-    tv_ref,
     ik_ref,
     iv_ref,
     qg_ref,
     kg_ref,
     xg_ref,
-    win_ref,
-    so_ref,
-    co_ref,
+    weights,
+    totals,
     text,
     text_out,
     keys,
@@ -220,6 +231,7 @@
     back_send,
     back_in,
     gaps,
+    local_sem,
     text_recv,
     up_send,
     down_send,
@@ -253,6 +265,31 @@
     def at_wid(target):
         return {"wid": target}
 
+    mine = pl.multiple_of(side * half, depth)
+    other = pl.multiple_of((1 - side) * half, depth)
+    loads = [
+        pltpu.make_async_copy(source, target, local_sem.at[at])
+        for at, (source, target) in enumerate(
+            (
+                (tk_hbm.at[:, pl.ds(mine, half)], text.at[0, w]),
+                (tk_hbm.at[:, pl.ds(other, half)], text_out.at[0]),
+                (tv_hbm.at[:, pl.ds(mine, half)], text.at[1, w]),
+                (tv_hbm.at[:, pl.ds(other, half)], text_out.at[1]),
+                (sq_hbm, sq_ref),
+                (sk_hbm, sk_ref),
+                (xq_hbm, xq_ref),
+                (sv_hbm, sv_ref),
+                (kg_hbm, kg_ref),
+                (xg_hbm, xg_ref),
+                (qg_hbm, qg_ref),
+                (ik_hbm, ik_ref),
+                (iv_hbm, iv_ref),
+            )
+        )
+    ]
+    for load in loads:
+        load.start()
+
     barrier = pltpu.get_barrier_semaphore()
     pl.semaphore_signal(barrier, inc=1, device_id={"tp": 1 - core}, device_id_type=MESH)
     for cond, target in (
@@ -266,66 +303,77 @@
         def _():
             pl.semaphore_signal(barrier, inc=1, device_id=at_wid(target), device_id_type=MESH)
 
-    mine = pl.multiple_of(side * half, depth)
-    other = pl.multiple_of((1 - side) * half, depth)
-    text[w, 0] = tk_ref[:, pl.ds(mine, half)]
-    text[w, 1] = tv_ref[:, pl.ds(mine, half)]
-    text_out[0] = tk_ref[:, pl.ds(other, half)]
-    text_out[1] = tv_ref[:, pl.ds(other, half)]
     expected = 1
     for cond in (not_first, not_last, has_down, has_up):
         expected = expected + jnp.where(cond, 1, 0)
     pl.semaphore_wait(barrier, expected)
 
-    def relay(slot, up):
+    def relay(kind, slot, up):
         return pltpu.make_async_remote_copy(
-            src_ref=text.at[slot],
-            dst_ref=text.at[slot],
-            send_sem=(up_send if up else down_send).at[slot],
-            recv_sem=text_recv.at[slot],
+            src_ref=text.at[kind, slot],
+            dst_ref=text.at[kind, slot],
+            send_sem=(up_send if up else down_send).at[kind, slot],
+            recv_sem=text_recv.at[kind, slot],
             device_id=at_wid(w + 2 if up else w - 2),
             device_id_type=MESH,
         )
 
-    def forward(slot, up):
+    def forward(kind, slot, up):
         @pl.when(has_up if up else has_down)
         def _():
-            relay(slot, up).start()
-
-    def take(slot):
+            relay(kind, slot, up).start()
+
+    def take(kind, slot):
         pltpu.make_async_remote_copy(
-            src_ref=text.at[slot],
-            dst_ref=text.at[slot],
-            send_sem=side_send,
-            recv_sem=text_recv.at[slot],
+            src_ref=text.at[kind, slot],
+            dst_ref=text.at[kind, slot],
+            send_sem=side_send.at[kind],
+            recv_sem=text_recv.at[kind, slot],
             device_id=at_wid(mate),
             device_id_type=MESH,
         ).wait_recv()
 
-    def relay_step(step, which):
+    def relay_step(kind, step, which):
         below, above = (line - step) * 2 + which, (line + step) * 2 + which
 
         @pl.when(line - step >= 0)
         def _():
-            take(below)
-            forward(below, True)
+            take(kind, below)
+            forward(kind, below, True)
 
         @pl.when(line + step < lines)
         def _():
-            take(above)
-            forward(above, False)
-
-    forward(w, True)
-    forward(w, False)
-    side_copy = pltpu.make_async_remote_copy(
-        src_ref=text_out,
-        dst_ref=text.at[w],
-        send_sem=side_send,
-        recv_sem=text_recv.at[w],
-        device_id=at_wid(mate),
-        device_id_type=MESH,
-    )
-    side_copy.start()
+            take(kind, above)
+            forward(kind, above, False)
+
+    steps = [
+        (step, side if turn == 0 else 1 - side) for step in range(1, lines - 1) for turn in range(2)
+    ]
+
+    def next_step():
+        if steps:
+            step, which = steps.pop(0)
+            for kind in range(2):
+                relay_step(kind, step, which)
+
+    side_copies = []
+    for kind in range(2):
+        loads[2 * kind].wait()
+        forward(kind, w, True)
+        forward(kind, w, False)
+        loads[2 * kind + 1].wait()
+        side_copy = pltpu.make_async_remote_copy(
+            src_ref=text_out.at[kind],
+            dst_ref=text.at[kind, w],
+            send_sem=side_send.at[kind],
+            recv_sem=text_recv.at[kind, w],
+            device_id=at_wid(mate),
+            device_id_type=MESH,
+        )
+        side_copy.start()
+        side_copies.append(side_copy)
+    for load in loads[4:11]:
+        load.wait()
 
     lane = lax.broadcasted_iota(jnp.int32, (tokens, depth), 1)
     sums = [squares_of(ref, head_count, depth, tokens) for ref in (sq_ref, sk_ref, xq_ref)]
@@ -340,6 +388,11 @@
     )
     stat_copy.start()
 
+    for kind in range(2):
+        take(kind, mate)
+        forward(kind, mate, True)
+        forward(kind, mate, False)
+
     place = lax.broadcasted_iota(jnp.int32, (tokens, tokens), 0)
     source = lax.broadcasted_iota(jnp.int32, (tokens, tokens), 1)
     inner = lax.rem(place, edge)
@@ -395,12 +448,13 @@
 
     def normed(ref, gain_ref, start, inverse_of):
         wide = head_block(ref, start, depth, tokens)
-        return (wide * inverse_of * gain_ref[:, pl.ds(start, depth)]).astype(jnp.bfloat16)
+        return (wide * inverse_of * gain_ref[pl.ds(start, depth)][None]).astype(jnp.bfloat16)
 
     for head in range(head_count):
         block = normed(sk_ref, kg_ref, head * depth, inverse_k)
         keys[edge : edge + tokens, head * depth : (head + 1) * depth] = tile_order(block)
     start_halo(keys, 0)
+    next_step()
 
     for head in range(half_heads):
         at = pl.multiple_of((1 - side) * half + head * depth, depth)
@@ -414,10 +468,6 @@
         device_id_type=MESH,
     )
     cross_copy.start()
-
-    take(mate)
-    forward(mate, True)
-    forward(mate, False)
 
     for head in range(half_heads):
         at = pl.multiple_of(side * half + head * depth, depth)
@@ -445,9 +495,9 @@
         queries = normed(sq_ref, qg_ref, head * depth, inverse_q)
         scores = dot_nt(queries, keys[:, at])
         allowed = (
-            (gaps[0] <= win_ref[head, 0])
-            & (gaps[1] <= win_ref[head, 1])
-            & (gaps[2] <= win_ref[head, 2])
+            (gaps[0] <= win_ref[0, head])
+            & (gaps[1] <= win_ref[1, head])
+            & (gaps[2] <= win_ref[2, head])
         )
         mixed = soft_mix(jnp.where(allowed, scores, masked), values[:, at], factor)
         so_ref[:, :, :, at] = mixed.reshape(frames, rows, cols, depth).astype(jnp.bfloat16)
@@ -458,20 +508,16 @@
         scores = dot_nt(cross[:, at], ik_ref[:, there])
         image_part[:, at] = soft_mix(scores, iv_ref[:, there], factor)
 
+    next_step()
     cross_copy.wait_recv()
-    steps = [(step, turn) for step in range(1, lines) for turn in range(2)]
-
-    def next_step():
-        if steps:
-            step, turn = steps.pop(0)
-            relay_step(step, side if turn == 0 else 1 - side)
-
-    next_step()
+    loads[11].wait()
+    loads[12].wait()
     for head in range(half_heads):
         image_head(head)
-        if head == half_heads // 2:
+        if head == half_heads // 2 - 1:
             next_step()
-    next_step()
+    while steps:
+        next_step()
 
     def wait_halo(ref, at):
         @pl.when(not_last)
@@ -486,17 +532,32 @@
     wait_halo(keys, 0)
     for head in range(head_count):
         self_head(head)
-        if head == head_count // 2 - 1:
-            next_step()
-    while steps:
-        next_step()
-
+
+    def last_step(kind):
+        if lines > 1:
+            for which in range(2):
+                relay_step(kind, lines - 1, which)
+
+    rows_all = wid_count * tk_hbm.shape[0]
+    last_step(0)
+    for head in range(half_heads):
+        at = slice(head * depth, (head + 1) * depth)
+        scores = dot_nt(cross[:, at], text[0, :, :, at].reshape(rows_all, depth))
+        row_top = jnp.max(scores, axis=-1, keepdims=True)
+        powers = jnp.exp((scores - row_top) * factor)
+        total = jnp.sum(powers, axis=-1, keepdims=True)
+        totals[:, at] = jnp.broadcast_to(1.0 / total, (2 * tokens, depth))
+        weights[head] = powers.astype(jnp.bfloat16)
+    last_step(1)
     backs = []
     for head in range(half_heads):
         at = slice(head * depth, (head + 1) * depth)
-        rows_all = wid_count * tk_ref.shape[0]
-        scores = dot_nt(cross[:, at], text[:, 0, :, at].reshape(rows_all, depth))
-        mixed = soft_mix(scores, text[:, 1, :, at].reshape(rows_all, depth), factor)
+        mixed = jnp.dot(
+            weights[head],
+            text[1, :, :, at].reshape(rows_all, depth),
+            preferred_element_type=jnp.float32,
+        )
+        mixed = mixed * totals[:, at]
         mixed = mixed + image_part[:, at]
         back_send[head] = mixed[tokens:].astype(jnp.bfloat16)
         back = pltpu.make_async_remote_copy(
@@ -513,7 +574,8 @@
         own = mixed[:tokens].reshape(frames, rows, cols, depth)
         co_ref[:, :, :, there] = own.astype(jnp.bfloat16)
 
-    side_copy.wait_send()
+    for side_copy in side_copies:
+        side_copy.wait_send()
     cross_copy.wait_send()
     for at, ref in ((0, keys), (2, values)):
 
@@ -531,11 +593,13 @@
 
             @pl.when(has_up & (place_line <= line))
             def _():
-                relay(slot, True).wait_send()
+                relay(0, slot, True).wait_send()
+                relay(1, slot, True).wait_send()
 
             @pl.when(has_down & (place_line >= line))
             def _():
-                relay(slot, False).wait_send()
+                relay(0, slot, False).wait_send()
+                relay(1, slot, False).wait_send()
 
     for head in range(half_heads):
         backs[head].wait()
@@ -576,10 +640,15 @@
             jax.ShapeDtypeStruct(self_query.shape, bf16),
             jax.ShapeDtypeStruct(self_query.shape, bf16),
         ),
-        in_specs=[vmem] * 11 + [pl.BlockSpec(memory_space=pltpu.SMEM)],
+        in_specs=[pl.BlockSpec(memory_space=pltpu.HBM)] * 11 + [pl.BlockSpec(memory_space=pltpu.SMEM)],
         out_specs=(vmem, vmem),
         scratch_shapes=[
-            pltpu.VMEM((wid_count, 2, text_rows, half), bf16),
+            *[pltpu.VMEM(self_query.shape, bf16)] * 4,
+            *[pltpu.VMEM(image_key.shape, bf16)] * 2,
+            *[pltpu.VMEM((channels,), f32)] * 3,
+            pltpu.VMEM((half_heads, 2 * tokens, wid_count * text_rows), bf16),
+            pltpu.VMEM((2 * tokens, half), f32),
+            pltpu.VMEM((2, wid_count, text_rows, half), bf16),
             pltpu.VMEM((2, text_rows, half), bf16),
             pltpu.VMEM((tokens + 2 * edge, channels), bf16),
             pltpu.VMEM((tokens + 2 * edge, channels), bf16),
@@ -591,10 +660,11 @@
             pltpu.VMEM((half_heads, tokens, depth), bf16),
             pltpu.VMEM((half_heads, tokens, depth), bf16),
             pltpu.VMEM((3, tokens, tokens + 2 * edge), jnp.int32),
-            dma((wid_count,)),
-            dma((wid_count,)),
-            dma((wid_count,)),
-            dma,
+            dma((13,)),
+            dma((2, wid_count)),
+            dma((2, wid_count)),
+            dma((2, wid_count)),
+            dma((2,)),
             dma((4,)),
             dma((4,)),
             dma,
@@ -604,7 +674,7 @@
             dma((half_heads,)),
         ],
         compiler_params=pltpu.CompilerParams(
-            collective_id=0, has_side_effects=True, vmem_limit_bytes=40 * 1024 * 1024
+            collective_id=0, has_side_effects=True, vmem_limit_bytes=56 * 1024 * 1024
         ),
         name="attention",
     )(
@@ -616,10 +686,10 @@
         text_value,
         image_key,
         image_value,
-        query_gain[None],
-        key_gain[None],
-        cross_gain[None],
-        windows,
+        query_gain,
+        key_gain,
+        cross_gain,
+        windows.T,
     )
 
 

time: 60 us -> 45.9 us (0.77)
  local copies, waits for them, and re-layouts: 11.5 us -> 2.49 us
  Pallas kernels: 47.3 us -> 42.6 us
    unnamed x25 -> x4, local copies, waits for them, and re-layouts: 10.8 us -> 2.49 us
    pallas_call x1, Pallas kernels: 47.3 us -> 42.6 us  [fused_body(): pl.pallas_call(functools.partial(fused, wid_count, head_count), out_shape...]
    broadcast_in_dim x3 -> x0, local copies, waits for them, and re-layouts: 0.72 us -> none  [the longest x1 0.71 us: fused_body(): query_gain[None]]
where the time goes in v2:
time: 45.9 us; the launch traced here: 45.7 us
  Pallas kernels  42.6 us (93%)
  local copies, waits for them, and re-layouts  2.49 us (5%)
  between operations  0.65 us (1%)
    pallas_call x1, Pallas kernels, fused_body(): pl.pallas_call(functools.partial(fused, wid_count, head_count), out_shape...  42.6 us
    unnamed x4, local copies, waits for them, and re-layouts  2.49 us

profile of v2, /device:TPU:0, one launch (start us, length us, event | category | flops | bytes accessed | tf_op | source)
XLA Modules:
  0.0 45.7 jit_solution(12708022396531866672)
XLA Ops:
  0.6 42.6 %attention.1 = (bf16[2,8,8,1280]{3,2,1,0:T(8,128)(2,1)}, bf16[2,8,8,1280]{3,2,1,0:T(8,128)(2,1)}) custom-call(bf16[2,8,8,1280]{3,2,1,0:T(8,128)(2,1)} %sq_hbm.1, bf16[2,8,8,1280]{3,2,1,0:T(8,128)(2,1)} %sk_hbm.1, bf16[2,8,8,1280]{3,2,1,0:T(8,128)(2,1)} %sv_hbm.1, bf16[2,8,8,1280]{3,2,1,0:T(8,128)(2,1)} %xq_hbm.1, bf16[64,1280]{1,0:T(8,128)(2,1)} %tk_hbm.1, ...), custom_call_target="tpu_custom_call" | custom-call | tf_op jit(solution)/shard_map/attention/pallas_call | solution.py:637
  43.2 0.0 copy-start
  43.2 1.8 %copy.16 = bf16[2,8,8,1280]{3,2,1,0:T(8,128)(2,1)} copy(bf16[2,8,8,1280]{3,2,1,0:T(8,128)(2,1)} %get-tuple-element.4) | data formatting | bytes 655360
  45.0 0.0 copy-done
  45.0 0.7 %copy.17 = bf16[2,8,8,1280]{3,2,1,0:T(8,128)(2,1)} copy(bf16[2,8,8,1280]{3,2,1,0:T(8,128)(2,1)S(1)} %copy-done) | data formatting | bytes 655360
Async XLA Ops:
  43.2 1.8 %copy-start = (bf16[2,8,8,1280]{3,2,1,0:T(8,128)(2,1)S(1)}, bf16[2,8,8,1280]{3,2,1,0:T(8,128)(2,1)}, u32[]{:S(2)}) copy-start(bf16[2,8,8,1280]{3,2,1,0:T(8,128)(2,1)} %get-tuple-element.5) | copy-start | bytes 983044

commit v3 on v2

--- a/solution.py
+++ b/solution.py
@@ -160,6 +160,7 @@
 
 
 MESH = pl.DeviceIdType.MESH
+GUESTS = 2
 
 
 def squares_of(ref, head_count, depth, tokens):
@@ -189,6 +190,10 @@
         powers.astype(jnp.bfloat16), value_rows, preferred_element_type=jnp.float32
     )
     return mixed * (1.0 / total)
+
+
+def guest_heads(wid_count, half_heads):
+    return GUESTS if wid_count >= 8 and half_heads > GUESTS else 0
 
 
 def fused(
@@ -219,6 +224,9 @@
     xg_ref,
     weights,
     totals,
+    guest_in,
+    guest_out,
+    guest_sem,
     text,
     text_out,
     keys,
@@ -253,6 +261,8 @@
     col_tiles = cols // TILE
     lines = wid_count // 2
     factor = 1.0 / math.sqrt(depth)
+    guests = guest_heads(wid_count, half_heads)
+    kept = half - guests * depth
 
     w = lax.axis_index("wid")
     core = lax.axis_index("tp")
@@ -261,6 +271,9 @@
     mate = line * 2 + (1 - side)
     not_first, not_last = w > 0, w < wid_count - 1
     has_down, has_up = line > 0, line < lines - 1
+    is_end = (line == 0) | (line == lines - 1)
+    is_host = (line == 1) | (line == lines - 2)
+    guest_peer = w + jnp.where((line == 0) | (line == lines - 2), 2, -2)
 
     def at_wid(target):
         return {"wid": target}
@@ -308,42 +321,61 @@
         expected = expected + jnp.where(cond, 1, 0)
     pl.semaphore_wait(barrier, expected)
 
-    def relay(kind, slot, up):
+    def slot_of(kind, slot, part):
+        if part:
+            return text.at[kind, slot, :, pl.ds(0, kept)]
+        return text.at[kind, slot]
+
+    def relay(kind, slot, up, part):
         return pltpu.make_async_remote_copy(
-            src_ref=text.at[kind, slot],
-            dst_ref=text.at[kind, slot],
+            src_ref=slot_of(kind, slot, part),
+            dst_ref=slot_of(kind, slot, part),
             send_sem=(up_send if up else down_send).at[kind, slot],
             recv_sem=text_recv.at[kind, slot],
             device_id=at_wid(w + 2 if up else w - 2),
             device_id_type=MESH,
         )
 
+    def with_relay(kind, slot, up, cond, act):
+        cond = cond & (has_up if up else has_down)
+        if guests == 0:
+            pl.when(cond)(lambda: act(relay(kind, slot, up, False)))
+            return
+        near = (line == lines - 2) if up else (line == 1)
+        pl.when(cond & near)(lambda: act(relay(kind, slot, up, True)))
+        pl.when(cond & jnp.logical_not(near))(lambda: act(relay(kind, slot, up, False)))
+
     def forward(kind, slot, up):
-        @pl.when(has_up if up else has_down)
-        def _():
-            relay(kind, slot, up).start()
-
-    def take(kind, slot):
+        with_relay(kind, slot, up, w >= 0, lambda copy: copy.start())
+
+    def take(kind, slot, part=False):
         pltpu.make_async_remote_copy(
-            src_ref=text.at[kind, slot],
-            dst_ref=text.at[kind, slot],
+            src_ref=slot_of(kind, slot, part),
+            dst_ref=slot_of(kind, slot, part),
             send_sem=side_send.at[kind],
             recv_sem=text_recv.at[kind, slot],
             device_id=at_wid(mate),
             device_id_type=MESH,
         ).wait_recv()
 
+    def take_line(kind, slot):
+        if guests == 0:
+            take(kind, slot)
+            return
+        pl.when(is_end)(lambda: take(kind, slot, True))
+        pl.when(jnp.logical_not(is_end))(lambda: take(kind, slot))
+
     def relay_step(kind, step, which):
         below, above = (line - step) * 2 + which, (line + step) * 2 + which
 
         @pl.when(line - step >= 0)
         def _():
-            take(kind, below)
+            take_line(kind, below)
             forward(kind, below, True)
 
         @pl.when(line + step < lines)
         def _():
-            take(kind, above)
+            take_line(kind, above)
             forward(kind, above, False)
 
     steps = [
@@ -510,6 +542,19 @@
 
     next_step()
     cross_copy.wait_recv()
+
+    def guest_copy(result):
+        return pltpu.make_async_remote_copy(
+            src_ref=guest_out if result else cross.at[:, pl.ds(kept, guests * depth)],
+            dst_ref=guest_in,
+            send_sem=guest_sem.at[2 if result else 0],
+            recv_sem=guest_sem.at[3 if result else 1],
+            device_id=at_wid(guest_peer),
+            device_id_type=MESH,
+        )
+
+    if guests:
+        pl.when(is_end)(lambda: guest_copy(False).start())
     loads[11].wait()
     loads[12].wait()
     for head in range(half_heads):
@@ -539,28 +584,31 @@
                 relay_step(kind, lines - 1, which)
 
     rows_all = wid_count * tk_hbm.shape[0]
-    last_step(0)
-    for head in range(half_heads):
-        at = slice(head * depth, (head + 1) * depth)
-        scores = dot_nt(cross[:, at], text[0, :, :, at].reshape(rows_all, depth))
+    def text_weights(queries, at):
+        scores = dot_nt(queries, text[0, :, :, at].reshape(rows_all, depth))
         row_top = jnp.max(scores, axis=-1, keepdims=True)
         powers = jnp.exp((scores - row_top) * factor)
         total = jnp.sum(powers, axis=-1, keepdims=True)
-        totals[:, at] = jnp.broadcast_to(1.0 / total, (2 * tokens, depth))
-        weights[head] = powers.astype(jnp.bfloat16)
-    last_step(1)
-    backs = []
-    for head in range(half_heads):
-        at = slice(head * depth, (head + 1) * depth)
-        mixed = jnp.dot(
-            weights[head],
+        return powers.astype(jnp.bfloat16), 1.0 / total
+
+    def text_mix(shares, at):
+        return jnp.dot(
+            shares,
             text[1, :, :, at].reshape(rows_all, depth),
             preferred_element_type=jnp.float32,
         )
-        mixed = mixed * totals[:, at]
-        mixed = mixed + image_part[:, at]
-        back_send[head] = mixed[tokens:].astype(jnp.bfloat16)
-        back = pltpu.make_async_remote_copy(
+
+    def columns(head):
+        return slice(head * depth, (head + 1) * depth)
+
+    def weigh(head):
+        at = columns(head)
+        shares, inverse_total = text_weights(cross[:, at], at)
+        totals[:, at] = jnp.broadcast_to(inverse_total, (2 * tokens, depth))
+        weights[head] = shares
+
+    def back(head):
+        return pltpu.make_async_remote_copy(
             src_ref=back_send.at[head],
             dst_ref=back_in.at[head],
             send_sem=back_send_sem.at[head],
@@ -568,11 +616,66 @@
             device_id=at_wid(mate),
             device_id_type=MESH,
         )
-        back.start()
-        backs.append(back)
+
+    def give(head, mixed):
+        back_send[head] = mixed[tokens:].astype(jnp.bfloat16)
+        back(head).start()
         there = pl.ds(pl.multiple_of(side * half + head * depth, depth), depth)
-        own = mixed[:tokens].reshape(frames, rows, cols, depth)
+        own = mixed[:tokens].astype(jnp.float32).reshape(frames, rows, cols, depth)
         co_ref[:, :, :, there] = own.astype(jnp.bfloat16)
+
+    def mix(head):
+        at = columns(head)
+        give(head, text_mix(weights[head], at) * totals[:, at] + image_part[:, at])
+
+    kept_heads = half_heads - guests
+    last_step(0)
+    for head in range(kept_heads):
+        weigh(head)
+    if guests:
+
+        @pl.when(jnp.logical_not(is_end))
+        def _():
+            for head in range(kept_heads, half_heads):
+                weigh(head)
+
+    last_step(1)
+    if guests:
+
+        @pl.when(is_host)
+        def _():
+            guest_copy(False).wait_recv()
+            for guest in range(guests):
+                at = columns(kept_heads + guest)
+                queries = guest_in[:, columns(guest)]
+                shares, inverse_total = text_weights(queries, at)
+                mixed = text_mix(shares, at) * inverse_total
+                first = side * half + (kept_heads + guest) * depth
+                there = pl.ds(pl.multiple_of(first, depth), depth)
+                scores = dot_nt(queries, ik_ref[:, there])
+                mixed = mixed + soft_mix(scores, iv_ref[:, there], factor)
+                guest_out[:, columns(guest)] = mixed.astype(jnp.bfloat16)
+            guest_copy(True).start()
+
+    for head in range(kept_heads):
+        mix(head)
+    if guests:
+
+        @pl.when(jnp.logical_not(is_end))
+        def _():
+            for head in range(kept_heads, half_heads):
+                mix(head)
+
+        @pl.when(is_end)
+        def _():
+            guest_copy(True).wait_recv()
+            for guest in range(guests):
+                give(kept_heads + guest, guest_in[:, columns(guest)])
+            guest_copy(False).wait_send()
+
+        @pl.when(is_host)
+        def _():
+            guest_copy(True).wait_send()
 
     for side_copy in side_copies:
         side_copy.wait_send()
@@ -591,18 +694,12 @@
         for place_side in range(2):
             slot = place_line * 2 + place_side
 
-            @pl.when(has_up & (place_line <= line))
-            def _():
-                relay(0, slot, True).wait_send()
-                relay(1, slot, True).wait_send()
-
-            @pl.when(has_down & (place_line >= line))
-            def _():
-                relay(0, slot, False).wait_send()
-                relay(1, slot, False).wait_send()
+            for kind in range(2):
+                with_relay(kind, slot, True, place_line <= line, lambda copy: copy.wait_send())
+                with_relay(kind, slot, False, place_line >= line, lambda copy: copy.wait_send())
 
     for head in range(half_heads):
-        backs[head].wait()
+        back(head).wait()
         there = pl.ds(pl.multiple_of((1 - side) * half + head * depth, depth), depth)
         came = back_in[head].astype(jnp.float32).reshape(frames, rows, cols, depth)
         co_ref[:, :, :, there] = came.astype(jnp.bfloat16)
@@ -631,6 +728,7 @@
     half = half_heads * depth
     edge = frames * rows * TILE
     text_rows = text_key.shape[0]
+    guests = guest_heads(wid_count, half_heads)
     bf16, f32 = jnp.bfloat16, jnp.float32
     dma = pltpu.SemaphoreType.DMA
     vmem = pl.BlockSpec(memory_space=pltpu.VMEM)
@@ -648,6 +746,8 @@
             *[pltpu.VMEM((channels,), f32)] * 3,
             pltpu.VMEM((half_heads, 2 * tokens, wid_count * text_rows), bf16),
             pltpu.VMEM((2 * tokens, half), f32),
+            *[pltpu.VMEM((2 * tokens, max(guests, 1) * depth), bf16)] * 2,
+            dma((4,)),
             pltpu.VMEM((2, wid_count, text_rows, half), bf16),
             pltpu.VMEM((2, text_rows, half), bf16),
             pltpu.VMEM((tokens + 2 * edge, channels), bf16),

time: 45.9 us -> 46 us (level)
  no operation moved by 1% of the time
where the time goes in v3:
time: 46 us; the launch traced here: 45.8 us
  Pallas kernels  42.7 us (93%)
  local copies, waits for them, and re-layouts  2.49 us (5%)
  between operations  0.65 us (1%)
    pallas_call x1, Pallas kernels, fused_body(): pl.pallas_call(functools.partial(fused, wid_count, head_count), out_shape...  42.7 us
    unnamed x4, local copies, waits for them, and re-layouts  2.49 us

profile of v3, /device:TPU:0, one launch (start us, length us, event | category | flops | bytes accessed | tf_op | source)
XLA Modules:
  0.0 45.8 jit_solution(9743342891536313047)
XLA Ops:
  0.6 42.7 %attention.1 = (bf16[2,8,8,1280]{3,2,1,0:T(8,128)(2,1)}, bf16[2,8,8,1280]{3,2,1,0:T(8,128)(2,1)}) custom-call(bf16[2,8,8,1280]{3,2,1,0:T(8,128)(2,1)} %sq_hbm.1, bf16[2,8,8,1280]{3,2,1,0:T(8,128)(2,1)} %sk_hbm.1, bf16[2,8,8,1280]{3,2,1,0:T(8,128)(2,1)} %sv_hbm.1, bf16[2,8,8,1280]{3,2,1,0:T(8,128)(2,1)} %xq_hbm.1, bf16[64,1280]{1,0:T(8,128)(2,1)} %tk_hbm.1, ...), custom_call_target="tpu_custom_call" | custom-call | tf_op jit(solution)/shard_map/attention/pallas_call | solution.py:735
  43.3 0.0 copy-start
  43.3 1.8 %copy.16 = bf16[2,8,8,1280]{3,2,1,0:T(8,128)(2,1)} copy(bf16[2,8,8,1280]{3,2,1,0:T(8,128)(2,1)} %get-tuple-element.4) | data formatting | bytes 655360
  45.1 0.0 copy-done
  45.1 0.7 %copy.17 = bf16[2,8,8,1280]{3,2,1,0:T(8,128)(2,1)} copy(bf16[2,8,8,1280]{3,2,1,0:T(8,128)(2,1)S(1)} %copy-done) | data formatting | bytes 655360
Async XLA Ops:
  43.3 1.8 %copy-start = (bf16[2,8,8,1280]{3,2,1,0:T(8,128)(2,1)S(1)}, bf16[2,8,8,1280]{3,2,1,0:T(8,128)(2,1)}, u32[]{:S(2)}) copy-start(bf16[2,8,8,1280]{3,2,1,0:T(8,128)(2,1)} %get-tuple-element.5) | copy-start | bytes 983044

commit v4 on v3

--- a/solution.py
+++ b/solution.py
@@ -227,6 +227,9 @@
     guest_in,
     guest_out,
     guest_sem,
+    passing,
+    transit_sem,
+    onward_sem,
     text,
     text_out,
     keys,
@@ -449,14 +452,40 @@
             device_id_type=MESH,
         )
 
+    to_line = jnp.where(side == 1, has_up, has_down)
+    from_line = jnp.where(side == 1, has_down, has_up)
+
+    def transit(ref, at):
+        return pltpu.make_async_remote_copy(
+            src_ref=ref.at[pl.ds(pl.multiple_of(jnp.where(side == 1, tokens, edge), 16), edge)],
+            dst_ref=passing.at[at // 2],
+            send_sem=transit_sem.at[at],
+            recv_sem=transit_sem.at[at + 1],
+            device_id=at_wid(jnp.where(side == 1, w + 2, w - 2)),
+            device_id_type=MESH,
+        )
+
+    def onward(ref, at):
+        start = pl.multiple_of(jnp.where(side == 1, 0, edge + tokens), 16)
+        return pltpu.make_async_remote_copy(
+            src_ref=passing.at[at // 2],
+            dst_ref=ref.at[pl.ds(start, edge)],
+            send_sem=onward_sem.at[at // 2],
+            recv_sem=halo_recv.at[jnp.where(side == 1, at + 1, at)],
+            device_id=at_wid(mate),
+            device_id_type=MESH,
+        )
+
+    def pass_on(ref, at):
+        @pl.when(from_line)
+        def _():
+            transit(ref, at).wait_recv()
+            onward(ref, at).start()
+
     def start_halo(ref, at):
-        @pl.when(not_first)
-        def _():
-            halo(ref, at, True).start()
-
-        @pl.when(not_last)
-        def _():
-            halo(ref, at + 1, False).start()
+        pl.when(to_line)(lambda: transit(ref, at).start())
+        pl.when(side == 1)(lambda: halo(ref, at, True).start())
+        pl.when(side == 0)(lambda: halo(ref, at + 1, False).start())
 
     @pl.when(w == 0)
     def _():
@@ -487,6 +516,7 @@
         keys[edge : edge + tokens, head * depth : (head + 1) * depth] = tile_order(block)
     start_halo(keys, 0)
     next_step()
+    pass_on(values, 2)
 
     for head in range(half_heads):
         at = pl.multiple_of((1 - side) * half + head * depth, depth)
@@ -500,6 +530,7 @@
         device_id_type=MESH,
     )
     cross_copy.start()
+    pass_on(keys, 0)
 
     for head in range(half_heads):
         at = pl.multiple_of(side * half + head * depth, depth)
@@ -682,13 +713,10 @@
     cross_copy.wait_send()
     for at, ref in ((0, keys), (2, values)):
 
-        @pl.when(not_first)
-        def _():
-            halo(ref, at, True).wait_send()
-
-        @pl.when(not_last)
-        def _():
-            halo(ref, at + 1, False).wait_send()
+        pl.when(to_line)(lambda: transit(ref, at).wait_send())
+        pl.when(from_line)(lambda: onward(ref, at).wait_send())
+        pl.when(side == 1)(lambda: halo(ref, at, True).wait_send())
+        pl.when(side == 0)(lambda: halo(ref, at + 1, False).wait_send())
 
     for place_line in range(lines):
         for place_side in range(2):
@@ -748,6 +776,9 @@
             pltpu.VMEM((2 * tokens, half), f32),
             *[pltpu.VMEM((2 * tokens, max(guests, 1) * depth), bf16)] * 2,
             dma((4,)),
+            pltpu.VMEM((2, edge, channels), bf16),
+            dma((4,)),
+            dma((2,)),
             pltpu.VMEM((2, wid_count, text_rows, half), bf16),
             pltpu.VMEM((2, text_rows, half), bf16),
             pltpu.VMEM((tokens + 2 * edge, channels), bf16),

time: 46 us -> 44.3 us (0.963)
  Pallas kernels: 42.7 us -> 41 us
    pallas_call x1, Pallas kernels: 42.7 us -> 41 us  [fused_body(): pl.pallas_call(functools.partial(fused, wid_count, head_count), out_shape...]
where the time goes in v4:
time: 44.3 us; the launch traced here: 44.1 us
  Pallas kernels  41 us (93%)
  local copies, waits for them, and re-layouts  2.49 us (6%)
  between operations  0.65 us (1%)
    pallas_call x1, Pallas kernels, fused_body(): pl.pallas_call(functools.partial(fused, wid_count, head_count), out_shape...  41 us
    unnamed x4, local copies, waits for them, and re-layouts  2.49 us

profile of v4, /device:TPU:0, one launch (start us, length us, event | category | flops | bytes accessed | tf_op | source)
XLA Modules:
  0.0 44.1 jit_solution(3695141841335487530)
XLA Ops:
  0.6 41.0 %attention.1 = (bf16[2,8,8,1280]{3,2,1,0:T(8,128)(2,1)}, bf16[2,8,8,1280]{3,2,1,0:T(8,128)(2,1)}) custom-call(bf16[2,8,8,1280]{3,2,1,0:T(8,128)(2,1)} %sq_hbm.1, bf16[2,8,8,1280]{3,2,1,0:T(8,128)(2,1)} %sk_hbm.1, bf16[2,8,8,1280]{3,2,1,0:T(8,128)(2,1)} %sv_hbm.1, bf16[2,8,8,1280]{3,2,1,0:T(8,128)(2,1)} %xq_hbm.1, bf16[64,1280]{1,0:T(8,128)(2,1)} %tk_hbm.1, ...), custom_call_target="tpu_custom_call" | custom-call | tf_op jit(solution)/shard_map/attention/pallas_call | solution.py:763
  41.6 0.0 copy-start
  41.6 1.8 %copy.16 = bf16[2,8,8,1280]{3,2,1,0:T(8,128)(2,1)} copy(bf16[2,8,8,1280]{3,2,1,0:T(8,128)(2,1)} %get-tuple-element.4) | data formatting | bytes 655360
  43.4 0.0 copy-done
  43.4 0.7 %copy.17 = bf16[2,8,8,1280]{3,2,1,0:T(8,128)(2,1)} copy(bf16[2,8,8,1280]{3,2,1,0:T(8,128)(2,1)S(1)} %copy-done) | data formatting | bytes 655360
Async XLA Ops:
  41.6 1.8 %copy-start = (bf16[2,8,8,1280]{3,2,1,0:T(8,128)(2,1)S(1)}, bf16[2,8,8,1280]{3,2,1,0:T(8,128)(2,1)}, u32[]{:S(2)}) copy-start(bf16[2,8,8,1280]{3,2,1,0:T(8,128)(2,1)} %get-tuple-element.5) | copy-start | bytes 983044
